TPU v7x, 32 devices: a whole 2x2x4 slice. The times are simulated.
32 devices in a mesh: row: 8 (over y, x, core), col: 4 (over z).
Axes of the slice: x: 2, y: 2, z: 4, core: 2. Of those that a mesh axis runs over, the one named last changes fastest.
Arguments:
- eigen_rows: float32 [1024, 65536], P(('col', 'row')), may hold values from -6 to 6
- householder: float32 [65536, 1024], P('row', 'col'), may hold values from -0.046875 to 0.046875
- owners: int32 [2], replicated, may hold values from 0 to 3, as said below
Outputs:
- vectors: float32 [1024, 65536], P('col', 'row')
Inputs may be any that keep to these rules, and one draw needn't show every extreme that they name: `owners`: 2 distinct block indices below 4.
All inputs are finite; a program needn't handle non-finite values.
Results may differ from a plain program's by a relative error of at most 0.0001.
Values sent between devices are 32-bit elements; how exact they have to be, the bound alone decides.
A program may use at most 192 MiB of HBM per device.

v0:
```python
import jax
import jax.numpy as jnp
from jax import lax
from jax.sharding import PartitionSpec as P

PANELS = 2


def broadcast(block, axis, owner):
    block = jnp.where(lax.axis_index(axis) == owner, block, jnp.zeros_like(block))
    return lax.psum(block, axis)


def shape_panel(stored, first_row, offset):
    rows = first_row + lax.broadcasted_iota(jnp.int32, stored.shape, 0)
    cols = offset + lax.broadcasted_iota(jnp.int32, stored.shape, 1)
    unit = jnp.where(rows == cols, jnp.ones_like(stored), jnp.zeros_like(stored))
    return jnp.where(rows > cols, stored, unit)


def matmul_full(left, right):
    return jnp.dot(left, right, precision=lax.Precision.HIGHEST)


def inverse_factor(gram):
    width = gram.shape[0]
    rows = lax.broadcasted_iota(jnp.int32, gram.shape, 0)
    cols = lax.broadcasted_iota(jnp.int32, gram.shape, 1)
    ident = jnp.where(rows == cols, jnp.ones_like(gram), jnp.zeros_like(gram))
    half_diag = jnp.sum(gram * ident, axis=1) * 0.5
    strict = jnp.where(cols > rows, gram, jnp.zeros_like(gram)) / half_diag[:, None]
    result = ident - strict
    power = strict
    reach = 2
    while reach < width:
        power = matmul_full(power, power)
        result = matmul_full(result, ident + power)
        reach = reach * 2
    return result / half_diag[None, :]


def solve_block(gram, inner):
    inverse = inverse_factor(gram)
    return lax.dot_general(
        inner, inverse, (((1,), (1,)), ((), ())), precision=lax.Precision.HIGHEST
    )


def gram_of(panel):
    return lax.dot_general(panel, panel, (((0,), (0,)), ((), ())), precision=lax.Precision.HIGHEST)


def reflect(current, panel):
    inner_part = jnp.dot(current, panel, precision=lax.Precision.HIGHEST)
    gram = None
    gram, inner = lax.psum((gram_of(panel), inner_part), "row")
    solved = solve_block(gram, inner)
    update = lax.dot_general(
        solved, panel, (((1,), (1,)), ((), ())), precision=lax.Precision.HIGHEST
    )
    return current - update


def on_device(eigen_rows, householder, owners):
    current = lax.all_to_all(eigen_rows, "row", split_axis=1, concat_axis=0, tiled=True)
    row_count = householder.shape[0]
    width = householder.shape[1]
    first_row = lax.axis_index("row") * row_count
    panels_here = []
    for panel_index in range(PANELS):
        stored = broadcast(householder, "col", owners[panel_index])
        panels_here.append(shape_panel(stored, first_row, panel_index * width))
    for panel_index in reversed(range(PANELS)):
        current = reflect(current, panels_here[panel_index])
    return current


def solution(mesh):
    return jax.shard_map(
        on_device,
        mesh=mesh,
        in_specs=(P(("col", "row"), None), P("row", "col"), P()),
        out_specs=P("col", "row"),
        check_vma=False,
    )
```

profile of v0, /device:TPU:1, one launch (start us, length us, event | category | flops | bytes accessed | tf_op | source)
XLA Modules:
  0.0 802.5 jit_solution(13446322576136521148)
XLA Ops:
  6.5 1.3 fusion.104
  9.2 10.2 %broadcast_select_fusion = (f32[8192,256]{1,0:T(8,128)}, f32[8192,256]{1,0:T(8,128)}) fusion(f32[8192,256]{1,0:T(8,128)} %param.4, pred[]{:T(512)S(6)} %eq.53, pred[]{:T(512)S(6)} %eq.50), kind=kLoop, calls=%fused_computation.22 | loop fusion | flops 4194304 | bytes 25165826 | tf_op jit(solution)/shard_map/jit(_where)/select_n | solution.py:10
  19.4 7.7 copy.7
  27.1 5.6 all-to-all-start
  32.7 552.2 %all-reduce.11.cloned.1.call-done = (f32[8192,256]{1,0:T(8,128)}, f32[8192,256]{1,0:T(8,128)}) async-done(((f32[8192,256]{1,0:T(8,128)}, f32[8192,256]{1,0:T(8,128)}), (f32[8192,256]{1,0:T(8,128)}, f32[8192,256]{1,0:T(8,128)})) %all-reduce.11.cloned.1.call-update) | async-done | bytes 16777232 | tf_op jit(solution)/shard_map/psum | solution.py:11
  584.9 23.1 %fusion = f32[256,256]{1,0:T(8,128)} fusion(f32[8192,256]{1,0:T(8,128)} %get-tuple-element.9, s32[256]{0:T(256)S(1)} %iota_add_fusion.1, s32[8192]{0:T(1024)S(1)} %iota_add_fusion), kind=kOutput, calls=%fused_computation.7 | convolution fusion | flops 6450839552 | bytes 8684544 | tf_op jit(solution)/shard_map/dot_general | solution.py:50
  608.0 21.5 %fusion.25 = f32[256,256]{0,1:T(8,128)} fusion(f32[256,8192]{1,0:T(8,128)} %bitcast.1, f32[8192,256]{1,0:T(8,128)} %get-tuple-element.9, s32[256]{0:T(256)S(1)} %iota_add_fusion.1, s32[8192]{0:T(1024)S(1)} %iota_add_fusion), kind=kOutput, calls=%fused_computation.54 | convolution fusion | flops 6450839552 | bytes 17073152 | tf_op jit(solution)/shard_map/dot_general | solution.py:54
  629.8 23.8 %fusion.2 = f32[256,256]{1,0:T(8,128)} fusion(f32[8192,256]{1,0:T(8,128)} %get-tuple-element.10, s32[8192]{0:T(1024)S(1)} %iota_add_fusion), kind=kOutput, calls=%fused_computation.9 | convolution fusion | flops 6450839552 | bytes 8683520 | tf_op jit(solution)/shard_map/dot_general | solution.py:50
  653.5 28.8 %all-reduce.9.cloned.1.call-done = (f32[256,256]{0,1:T(8,128)}, f32[256,256]{1,0:T(8,128)}) async-done(((f32[256,256]{0,1:T(8,128)}, f32[256,256]{1,0:T(8,128)}), (f32[256,256]{0,1:T(8,128)}, f32[256,256]{1,0:T(8,128)})) %all-reduce.9.cloned.1.call-update) | async-done | bytes 524304 | tf_op jit(solution)/shard_map/psum | solution.py:56
  682.3 1.1 fusion.26
  683.4 1.5 fusion.64
  685.4 1.4 fusion.27
  688.7 0.4 fusion.30
  691.1 0.6 fusion.110
  691.7 13.6 %convolution_subtract_fusion.1 = f32[256,8192]{1,0:T(8,128)S(1)} fusion(f32[256,8192]{1,0:T(8,128)} %bitcast.1, f32[256,256]{1,0:T(8,128)S(1)} %fusion.110, f32[8192,256]{1,0:T(8,128)} %get-tuple-element.9, s32[256]{0:T(256)S(1)} %iota_add_fusion.1, s32[8192]{0:T(1024)S(1)} %iota_add_fusion), kind=kOutput, calls=%fused_computation.1 | convolution fusion | flops 6452936704 | bytes 25461760 | tf_op jit(solution)/shard_map/dot_general | solution.py:58
  705.4 3.4 copy-done
  708.8 8.9 %fusion.3 = f32[256,256]{1,0:T(8,128)} fusion(f32[256,8192]{1,0:T(8,128)S(1)} %convolution_subtract_fusion.1, f32[8192,256]{1,0:T(8,128)S(1)} %bitcast.58, s32[8192]{0:T(1024)S(1)} %iota_add_fusion), kind=kOutput, calls=%fused_computation.10 | convolution fusion | flops 6450839552 | bytes 17072128 | tf_op jit(solution)/shard_map/dot_general | solution.py:54
  717.7 54.1 %all-reduce.7.cloned.1.call-done = (f32[256,256]{1,0:T(8,128)}, f32[256,256]{1,0:T(8,128)}) async-done(((f32[256,256]{1,0:T(8,128)}, f32[256,256]{1,0:T(8,128)}), (f32[256,256]{1,0:T(8,128)}, f32[256,256]{1,0:T(8,128)})) %all-reduce.7.cloned.1.call-update) | async-done | bytes 524304 | tf_op jit(solution)/shard_map/psum | solution.py:56
  771.8 1.2 fusion.33
  773.0 2.1 fusion.65
  775.5 1.4 fusion.34
  779.7 0.6 fusion.38
  781.5 0.4 fusion.116
  781.9 13.8 %convolution_subtract_fusion = f32[256,8192]{1,0:T(8,128)} fusion(f32[256,8192]{1,0:T(8,128)S(1)} %copy-done.1, f32[256,256]{1,0:T(8,128)S(1)} %fusion.116, f32[8192,256]{1,0:T(8,128)} %get-tuple-element.10, s32[8192]{0:T(1024)S(1)} %iota_add_fusion), kind=kOutput, calls=%fused_computation | convolution fusion | flops 6452936704 | bytes 25460736 | tf_op jit(solution)/shard_map/dot_general | solution.py:58
  (45 shorter events, 8.8 us)
Async XLA Ops:
  6.5 578.3 %all-reduce.11.cloned.1.call-start = ((), (), s32[]{:S(2)}) async-start(), calls=%async_computation.3 | async-start | bytes 33554432 | tf_op jit(solution)/shard_map/psum | solution.py:11
  27.1 580.9 %all-to-all-start = ((f32[32,8,8192]{2,0,1:T(8,128)}), f32[32,8,8192]{2,0,1:T(8,128)}, u32[]{:S(2)}, u32[]{:S(2)}) async-start(f32[32,8,8192]{2,0,1:T(8,128)} %bitcast.59), calls=%async_computation | async-start | bytes 16777216 | tf_op jit(solution)/shard_map/all_to_all | solution.py:65
  32.6 649.7 %all-reduce.9.cloned.1.call-start = ((), (), s32[]{:S(2)}) async-start(), calls=%async_computation.2 | async-start | bytes 1048576 | tf_op jit(solution)/shard_map/psum | solution.py:56
  629.5 142.3 %all-reduce.7.cloned.1.call-start = ((), (), s32[]{:S(2)}) async-start(), calls=%async_computation.1 | async-start | bytes 1048576 | tf_op jit(solution)/shard_map/psum | solution.py:56
  682.3 8.8 %copy-start.2 = (f32[256,256]{0,1:T(8,128)S(1)}, f32[256,256]{0,1:T(8,128)}, u32[]{:S(2)}) copy-start(f32[256,256]{0,1:T(8,128)} %get-tuple-element.7) | copy-start | bytes 786436
  690.7 18.0 %slice-start = ((s8[8388608]{0:T(1024)(128)(4,1)}), s8[4194304]{0:T(1024)(128)(4,1)S(1)}, s32[]{:S(2)}) async-start(s8[8388608]{0:T(1024)(128)(4,1)} %bitcast.57), calls=%async_computation.4 | async-start | bytes 8388608
  691.7 17.0 %slice-start.1 = ((s8[8388608]{0:T(1024)(128)(4,1)}), s8[4194304]{0:T(1024)(128)(4,1)S(1)}, s32[]{:S(2)}) async-start(s8[8388608]{0:T(1024)(128)(4,1)} %bitcast.57), calls=%async_computation.5 | async-start | bytes 8388608
  705.4 3.4 copy-start
  771.8 9.7 %copy-start.3 = (f32[256,256]{1,0:T(8,128)S(1)}, f32[256,256]{1,0:T(8,128)}, u32[]{:S(2)}) copy-start(f32[256,256]{1,0:T(8,128)} %get-tuple-element.5) | copy-start | bytes 786436
  771.8 10.1 %copy-start.1 = (f32[256,8192]{1,0:T(8,128)S(1)}, f32[256,8192]{1,0:T(8,128)}, u32[]{:S(2)}) copy-start(f32[256,8192]{1,0:T(8,128)} %copy-done) | copy-start | bytes 25165828
Sparse Core Ops, SparseCore 0:
  19.5 565.3 all-reduce.10
  629.7 52.6 all-reduce.8
  717.8 53.9 all-reduce.6
where the time goes:
time: 814 us; the launch traced here: 802 us
  waiting for transfers between devices  635 us (78%)
  matrix products  122 us (15%)
  between operations  14.9 us (2%)
  other arithmetic  12.5 us (2%)
  local copies, waits for them, and re-layouts  12.4 us (2%)
    psum x1, waiting for transfers between devices, broadcast(): return lax.psum(block, axis)  552 us
    psum x2, waiting for transfers between devices, reflect(): gram, inner = lax.psum((gram_of(panel), inner_part), 'row')  82.9 us
    dot_general x2, matrix products, gram_of(): lax.dot_general(panel, panel, (((0,), (0,)), ((), ())), precision=lax.Pre...  46.9 us
    dot_general x2, matrix products, reflect(): inner_part = jnp.dot(current, panel, precision=lax.Precision.HIGHEST)  30.4 us
    dot_general x2, matrix products, reflect(): lax.dot_general(solved, panel, (((1,), (1,)), ((), ())), precision=lax.Pr...  27.4 us
  transfers between devices with their start and end apart: 4, of which 3 were waited for; matrix products, arithmetic and copies ran while one was open for 7% of the time, Pallas kernels for 0%

commit v1 on v0

v1 whole, which is shorter than its diff:
```python
import functools

import jax
import jax.numpy as jnp
from jax import lax
from jax.experimental import pallas as pl
from jax.experimental.pallas import tpu as pltpu
from jax.sharding import PartitionSpec as P

PANELS = 2
MESH = pl.DeviceIdType.MESH
FULL = lax.Precision.HIGHEST


def dot(left, right, left_dim=1, right_dim=0):
    return lax.dot_general(
        left, right, (((left_dim,), (right_dim,)), ((), ())),
        precision=FULL, preferred_element_type=jnp.float32,
    )


def inverse_factor(gram):
    width = gram.shape[0]
    rows = lax.broadcasted_iota(jnp.int32, gram.shape, 0)
    cols = lax.broadcasted_iota(jnp.int32, gram.shape, 1)
    ident = jnp.where(rows == cols, 1.0, 0.0)
    half_down = jnp.sum(gram * ident, axis=1, keepdims=True) * 0.5
    half_across = jnp.sum(gram * ident, axis=0, keepdims=True) * 0.5
    strict = jnp.where(cols > rows, gram, 0.0) / half_down
    result = ident - strict
    power = strict
    reach = 2
    while reach < width:
        power = dot(power, power)
        result = dot(result, ident + power)
        reach = reach * 2
    return result / half_across


def kernel(
    row_n, col_n, chunk, exchange, eigen_ref, house_ref, flag_ref, out_ref,
    right_buf, left_buf, own, current, acc, parts, full, solved,
    right_send, right_recv, left_send, left_recv,
    swap_send, swap_recv, part_send, part_recv, full_send, full_recv, own_sem, here_sem, out_sem,
):
    row = lax.axis_index("row")
    col = lax.axis_index("col")
    row_count, width = own.shape
    mine_rows = current.shape[0]
    per_panel = row_count // chunk
    total = PANELS * per_panel
    share = parts.shape[1]
    grams = PANELS + 1

    own_copy = pltpu.make_async_copy(house_ref, own, own_sem)
    own_copy.start()
    if exchange:
        give = eigen_ref.shape[0]
        here = pltpu.make_async_copy(
            eigen_ref.at[:, pl.ds(pl.multiple_of(row * row_count, 128), row_count)],
            current.at[pl.ds(pl.multiple_of(row * give, 8), give), :], here_sem,
        )
    else:
        here = pltpu.make_async_copy(eigen_ref, current, here_sem)
    here.start()

    barrier = pltpu.get_barrier_semaphore()
    for step in range(1, row_n):
        pl.semaphore_signal(
            barrier, inc=1, device_id=(lax.rem(row + step, row_n), col), device_id_type=MESH)

    @pl.when(col > 0)
    def _():
        pl.semaphore_signal(barrier, inc=1, device_id=(row, col - 1), device_id_type=MESH)

    @pl.when(col < col_n - 1)
    def _():
        pl.semaphore_signal(barrier, inc=1, device_id=(row, col + 1), device_id_type=MESH)

    beside = jnp.where(col > 0, 1, 0) + jnp.where(col < col_n - 1, 1, 0)
    pl.semaphore_wait(barrier, row_n - 1 + beside)

    def swap(step):
        peer = lax.rem(row + step, row_n)
        return pltpu.make_async_remote_copy(
            src_ref=eigen_ref.at[:, pl.ds(pl.multiple_of(peer * row_count, 128), row_count)],
            dst_ref=current.at[pl.ds(pl.multiple_of(row * give, 8), give), :],
            send_sem=swap_send.at[step], recv_sem=swap_recv.at[step],
            device_id=(peer, col), device_id_type=MESH,
        )

    if exchange:
        for step in range(1, row_n):
            swap(step).start()
    own_copy.wait()

    def piece(index):
        return pl.ds(pl.multiple_of(index * chunk, chunk), chunk)

    def to_right(index):
        at = piece(index)
        return pltpu.make_async_remote_copy(
            src_ref=right_buf.at[at, :], dst_ref=right_buf.at[at, :],
            send_sem=right_send.at[index], recv_sem=right_recv.at[index],
            device_id=(row, lax.rem(col + 1, col_n)), device_id_type=MESH,
        )

    def to_left(index):
        at = piece(index)
        return pltpu.make_async_remote_copy(
            src_ref=left_buf.at[at, :], dst_ref=left_buf.at[at, :],
            send_sem=left_send.at[index], recv_sem=left_recv.at[index],
            device_id=(row, lax.rem(col + col_n - 1, col_n)), device_id_type=MESH,
        )

    def flag(index):
        return jnp.broadcast_to(flag_ref[pl.ds(index, 1), :], (chunk, width)) > 0

    def pass_on(index, buf, copy, first, last):
        at = piece(index)
        panel = index // per_panel
        stored = own[piece(lax.rem(index, per_panel)), :]

        @pl.when(first)
        def _():
            buf[at, :] = stored

        @pl.when(jnp.logical_not(first))
        def _():
            copy(index).wait_recv()
            buf[at, :] = jnp.where(flag(panel), stored, buf[at, :])

        @pl.when(jnp.logical_not(last))
        def _():
            copy(index).start()

    def reflectors(panel, block):
        at = piece(panel * per_panel + block)
        stored = jnp.where(flag(PANELS + panel), right_buf[at, :], left_buf[at, :])
        rows = row * row_count + block * chunk + lax.broadcasted_iota(jnp.int32, stored.shape, 0)
        cols = (PANELS - 1 - panel) * width + lax.broadcasted_iota(jnp.int32, stored.shape, 1)
        return jnp.where(rows > cols, stored, jnp.where(rows == cols, 1.0, 0.0))

    def add(start, size, value):
        acc[start:start + size, :] = acc[start:start + size, :] + value

    acc[...] = jnp.zeros_like(acc)
    from_left = col
    from_right = col_n - 1 - col

    @pl.loop(0, total + 2 * (col_n - 1))
    def _(step):
        index_right = step - 2 * from_left

        @pl.when(jnp.logical_and(index_right >= 0, index_right < total))
        def _():
            pass_on(index_right, right_buf, to_right, col == 0, col == col_n - 1)

        index_left = step - 2 * from_right

        @pl.when(jnp.logical_and(index_left >= 0, index_left < total))
        def _():
            pass_on(index_left, left_buf, to_left, col == col_n - 1, col == 0)

        index = step - 2 * jnp.maximum(from_left, from_right)

        @pl.when(jnp.logical_and(index >= 0, index < per_panel))
        def _():
            panel = reflectors(0, index)
            add(0, width, dot(panel, panel, 0, 0))

        @pl.when(index == per_panel)
        def _():
            here.wait()
            if exchange:
                for other in range(1, row_n):
                    swap(other).wait_recv()

        @pl.when(jnp.logical_and(index >= per_panel, index < total))
        def _():
            block = index - per_panel
            first = reflectors(0, block)
            second = reflectors(1, block)
            held = current[:, piece(block)]
            add(width, width, dot(second, second, 0, 0))
            add(2 * width, width, dot(first, second, 0, 0))
            add(grams * width, mine_rows, dot(held, first))
            add(grams * width + mine_rows, mine_rows, dot(held, second))

    def part(index):
        return pl.ds(pl.multiple_of(index * share, 8), share)

    def part_copy(step):
        peer = lax.rem(row + step, row_n)
        return pltpu.make_async_remote_copy(
            src_ref=acc.at[part(peer), :], dst_ref=parts.at[step],
            send_sem=part_send.at[step], recv_sem=part_recv.at[step],
            device_id=(peer, col), device_id_type=MESH,
        )

    def full_copy(step):
        return pltpu.make_async_remote_copy(
            src_ref=full.at[part(row), :], dst_ref=full.at[part(row), :],
            send_sem=full_send.at[step], recv_sem=full_recv.at[step],
            device_id=(lax.rem(row + step, row_n), col), device_id_type=MESH,
        )

    for step in range(1, row_n):
        part_copy(step).start()
    summed = acc[part(row), :]
    for step in range(1, row_n):
        part_copy(step).wait_recv()
        summed = summed + parts[step]
    full[part(row), :] = summed
    for step in range(1, row_n):
        full_copy(step).start()
    for step in range(1, row_n):
        full_copy(step).wait_recv()

    inner = grams * width
    inverse_first = inverse_factor(full[0:width, :])
    inverse_second = inverse_factor(full[width:2 * width, :])
    solved_first = dot(full[inner:inner + mine_rows, :], inverse_first, 1, 1)
    inner_second = full[inner + mine_rows:inner + 2 * mine_rows, :] - dot(
        solved_first, full[2 * width:3 * width, :])
    solved[0] = solved_first
    solved[1] = dot(inner_second, inverse_second, 1, 1)

    def out_copy(block):
        at = piece(block)
        return pltpu.make_async_copy(current.at[:, at], out_ref.at[:, at], out_sem.at[block])

    @pl.loop(0, per_panel)
    def _(block):
        update = dot(solved[0], reflectors(0, block), 1, 1) + dot(
            solved[1], reflectors(1, block), 1, 1)
        at = piece(block)
        current[:, at] = current[:, at] - update
        out_copy(block).start()

    @pl.loop(0, total)
    def _(index):
        @pl.when(col < col_n - 1)
        def _():
            to_right(index).wait_send()

        @pl.when(col > 0)
        def _():
            to_left(index).wait_send()

    for step in range(1, row_n):
        if exchange:
            swap(step).wait_send()
        part_copy(step).wait_send()
        full_copy(step).wait_send()

    @pl.loop(0, per_panel)
    def _(block):
        out_copy(block).wait()


def on_device(row_n, col_n, eigen_rows, householder, owners):
    row_count, width = householder.shape
    give = eigen_rows.shape[0]
    mine_rows = give * row_n
    exchange = give % 8 == 0
    if not exchange:
        eigen_rows = lax.all_to_all(eigen_rows, "row", split_axis=1, concat_axis=0, tiled=True)
    chunk = min(256, row_count)
    per_panel = row_count // chunk
    total = PANELS * per_panel
    col = lax.axis_index("col")
    order = owners[::-1]
    flags = jnp.concatenate([order == col, order <= col]).astype(jnp.int32)
    flags = jnp.broadcast_to(
        jnp.pad(flags, (0, 8 - 2 * PANELS))[:, None], (8, width))
    rows = (PANELS + 1) * width + PANELS * mine_rows
    share = -(-rows // (8 * row_n)) * 8
    dma = pltpu.SemaphoreType.DMA
    return pl.pallas_call(
        functools.partial(kernel, row_n, col_n, chunk, exchange),
        out_shape=jax.ShapeDtypeStruct((mine_rows, row_count), jnp.float32),
        in_specs=[
            pl.BlockSpec(memory_space=pl.ANY),
            pl.BlockSpec(memory_space=pl.ANY),
            pl.BlockSpec(memory_space=pltpu.VMEM),
        ],
        out_specs=pl.BlockSpec(memory_space=pl.ANY),
        scratch_shapes=[
            pltpu.VMEM((PANELS * row_count, width), jnp.float32),
            pltpu.VMEM((PANELS * row_count, width), jnp.float32),
            pltpu.VMEM((row_count, width), jnp.float32),
            pltpu.VMEM((mine_rows, row_count), jnp.float32),
            pltpu.VMEM((share * row_n, width), jnp.float32),
            pltpu.VMEM((row_n, share, width), jnp.float32),
            pltpu.VMEM((share * row_n, width), jnp.float32),
            pltpu.VMEM((PANELS, mine_rows, width), jnp.float32),
            dma((total,)), dma((total,)), dma((total,)), dma((total,)),
            dma((row_n,)), dma((row_n,)), dma((row_n,)), dma((row_n,)),
            dma((row_n,)), dma((row_n,)),
            dma, dma, dma((per_panel,)),
        ],
        compiler_params=pltpu.CompilerParams(
            collective_id=0, has_side_effects=True, vmem_limit_bytes=60 * 2**20),
    )(eigen_rows, householder, flags)


def solution(mesh):
    return jax.shard_map(
        functools.partial(on_device, mesh.shape["row"], mesh.shape["col"]),
        mesh=mesh,
        in_specs=(P(("col", "row"), None), P("row", "col"), P()),
        out_specs=P("col", "row"),
        check_vma=False,
    )
```

time: 814 us -> 463 us (0.57); the launches traced: 802 us -> 463 us
  waiting for transfers between devices: 635 us -> 0 us
  Pallas kernels: 0 us -> 453 us
  matrix products: 122 us -> 0 us
  between operations: 14.9 us -> 0.01 us
  other arithmetic: 12.5 us -> 0.09 us
    psum x3 -> x0, waiting for transfers between devices: 635 us -> none  [the longest x1 552 us: broadcast(): return lax.psum(block, axis)]
    pallas_call x0 -> x1, Pallas kernels: none -> 453 us  [on_device(): pl.pallas_call(functools.partial(kernel, row_n, col_n, chunk, exchange),...]
    dot_general x36 -> x0, matrix products: 122 us -> none  [the longest x2 46.9 us: gram_of(): lax.dot_general(panel, panel, (((0,), (0,)), ((), ())), precision=lax.Pre...]
    select_n x1 -> x0, other arithmetic: 10.2 us -> none  [broadcast(): jnp.where(lax.axis_index(axis) == owner, block, jnp.zeros_like(block))]
  transfers between devices with their start and end apart: 4 -> 0, of which waited for: 3 -> 0; matrix products, arithmetic and copies ran while one was open for 7% -> 0% of each run, Pallas kernels for 0% -> 0%
where the time goes in v1:
time: 463 us
  Pallas kernels  453 us (98%)
  local copies, waits for them, and re-layouts  9.1 us (2%)
    pallas_call x1, Pallas kernels, on_device(): pl.pallas_call(functools.partial(kernel, row_n, col_n, chunk, exchange),...  453 us

profile of v1, /device:TPU:1, one launch (start us, length us, event | category | flops | bytes accessed | tf_op | source)
XLA Modules:
  0.0 462.5 jit_solution(13914363152509937035)
XLA Ops:
  0.0 0.7 rev.3
  0.8 0.1 pad_add_fusion
  0.8 0.7 broadcast_in_dim.2.flag_ref
  1.5 453.3 %shard_map.37 = f32[256,8192]{1,0:T(8,128)} custom-call(f32[32,65536]{1,0:T(8,128)} %eigen_ref.1, f32[8192,256]{1,0:T(8,128)} %house_ref.1, s32[8,256]{1,0:T(8,128)} %broadcast_in_dim.2.flag_ref), custom_call_target="tpu_custom_call" | custom-call | tf_op jit(solution)/shard_map/pallas_call | solution.py:280
  454.8 7.7 %copy.5 = f32[256,8192]{1,0:T(8,128)} copy(f32[256,8192]{1,0:T(8,128)} %shard_map.37) | data formatting | bytes 16777216
  (2 shorter events, 0.0 us)

commit v2 on v1

--- a/solution.py
+++ b/solution.py
@@ -17,6 +17,23 @@
         left, right, (((left_dim,), (right_dim,)), ((), ())),
         precision=FULL, preferred_element_type=jnp.float32,
     )
+
+
+def halves(value):
+    high = value.astype(jnp.bfloat16)
+    return high, (value - high.astype(jnp.float32)).astype(jnp.bfloat16)
+
+
+def dot_halves(left, right, left_dim=1, right_dim=0):
+    def one(a, b):
+        return lax.dot_general(
+            a, b, (((left_dim,), (right_dim,)), ((), ())), preferred_element_type=jnp.float32)
+
+    return one(left[0], right[0]) + (one(left[0], right[1]) + one(left[1], right[0]))
+
+
+def dot_split(left, right, left_dim=1, right_dim=0):
+    return dot_halves(halves(left), halves(right), left_dim, right_dim)
 
 
 def inverse_factor(gram):
@@ -31,8 +48,8 @@
     power = strict
     reach = 2
     while reach < width:
-        power = dot(power, power)
-        result = dot(result, ident + power)
+        power = dot_split(power, power)
+        result = result + dot_split(result, power)
         reach = reach * 2
     return result / half_across
 
@@ -49,8 +66,7 @@
     mine_rows = current.shape[0]
     per_panel = row_count // chunk
     total = PANELS * per_panel
-    share = parts.shape[1]
-    grams = PANELS + 1
+    share = parts.shape[2]
 
     own_copy = pltpu.make_async_copy(house_ref, own, own_sem)
     own_copy.start()
@@ -141,12 +157,53 @@
         cols = (PANELS - 1 - panel) * width + lax.broadcasted_iota(jnp.int32, stored.shape, 1)
         return jnp.where(rows > cols, stored, jnp.where(rows == cols, 1.0, 0.0))
 
-    def add(start, size, value):
-        acc[start:start + size, :] = acc[start:start + size, :] + value
+    def add(panel, start, size, value):
+        acc[panel, start:start + size, :] = acc[panel, start:start + size, :] + value
+
+    def add_inner(panel, block):
+        add(panel, width, mine_rows, dot(current[:, piece(block)], reflectors(panel, block)))
+
+    def part(index):
+        return pl.ds(pl.multiple_of(index * share, 8), share)
+
+    def part_copy(panel, step):
+        peer = lax.rem(row + step, row_n)
+        return pltpu.make_async_remote_copy(
+            src_ref=acc.at[panel, part(peer), :], dst_ref=parts.at[panel, step],
+            send_sem=part_send.at[panel, step], recv_sem=part_recv.at[panel, step],
+            device_id=(peer, col), device_id_type=MESH,
+        )
+
+    def full_copy(panel, step):
+        return pltpu.make_async_remote_copy(
+            src_ref=full.at[panel, part(row), :], dst_ref=full.at[panel, part(row), :],
+            send_sem=full_send.at[panel, step], recv_sem=full_recv.at[panel, step],
+            device_id=(lax.rem(row + step, row_n), col), device_id_type=MESH,
+        )
+
+    def give_parts(panel):
+        for step in range(1, row_n):
+            part_copy(panel, step).start()
+
+    def give_sums(panel):
+        summed = acc[panel, part(row), :]
+        for step in range(1, row_n):
+            part_copy(panel, step).wait_recv()
+            summed = summed + parts[panel, step]
+        full[panel, part(row), :] = summed
+        for step in range(1, row_n):
+            full_copy(panel, step).start()
+
+    def solve(panel):
+        for step in range(1, row_n):
+            full_copy(panel, step).wait_recv()
+        inverse = inverse_factor(full[panel, 0:width, :])
+        solved[panel] = dot_split(full[panel, width:width + mine_rows, :], inverse, 1, 1)
 
     acc[...] = jnp.zeros_like(acc)
     from_left = col
     from_right = col_n - 1 - col
+    late = per_panel - per_panel // 4
 
     @pl.loop(0, total + 2 * (col_n - 1))
     def _(step):
@@ -167,64 +224,56 @@
         @pl.when(jnp.logical_and(index >= 0, index < per_panel))
         def _():
             panel = reflectors(0, index)
-            add(0, width, dot(panel, panel, 0, 0))
-
-        @pl.when(index == per_panel)
+            add(0, 0, width, dot(panel, panel, 0, 0))
+
+        @pl.when(index == late)
         def _():
             here.wait()
             if exchange:
                 for other in range(1, row_n):
                     swap(other).wait_recv()
 
-        @pl.when(jnp.logical_and(index >= per_panel, index < total))
-        def _():
-            block = index - per_panel
-            first = reflectors(0, block)
-            second = reflectors(1, block)
-            held = current[:, piece(block)]
-            add(width, width, dot(second, second, 0, 0))
-            add(2 * width, width, dot(first, second, 0, 0))
-            add(grams * width, mine_rows, dot(held, first))
-            add(grams * width + mine_rows, mine_rows, dot(held, second))
-
-    def part(index):
-        return pl.ds(pl.multiple_of(index * share, 8), share)
-
-    def part_copy(step):
-        peer = lax.rem(row + step, row_n)
-        return pltpu.make_async_remote_copy(
-            src_ref=acc.at[part(peer), :], dst_ref=parts.at[step],
-            send_sem=part_send.at[step], recv_sem=part_recv.at[step],
-            device_id=(peer, col), device_id_type=MESH,
-        )
-
-    def full_copy(step):
-        return pltpu.make_async_remote_copy(
-            src_ref=full.at[part(row), :], dst_ref=full.at[part(row), :],
-            send_sem=full_send.at[step], recv_sem=full_recv.at[step],
-            device_id=(lax.rem(row + step, row_n), col), device_id_type=MESH,
-        )
-
-    for step in range(1, row_n):
-        part_copy(step).start()
-    summed = acc[part(row), :]
-    for step in range(1, row_n):
-        part_copy(step).wait_recv()
-        summed = summed + parts[step]
-    full[part(row), :] = summed
-    for step in range(1, row_n):
-        full_copy(step).start()
-    for step in range(1, row_n):
-        full_copy(step).wait_recv()
-
-    inner = grams * width
-    inverse_first = inverse_factor(full[0:width, :])
-    inverse_second = inverse_factor(full[width:2 * width, :])
-    solved_first = dot(full[inner:inner + mine_rows, :], inverse_first, 1, 1)
-    inner_second = full[inner + mine_rows:inner + 2 * mine_rows, :] - dot(
-        solved_first, full[2 * width:3 * width, :])
-    solved[0] = solved_first
-    solved[1] = dot(inner_second, inverse_second, 1, 1)
+        @pl.when(jnp.logical_and(index >= late, index < per_panel))
+        def _():
+            @pl.loop(0, 4)
+            def _(more):
+                add_inner(0, (index - late) * 4 + more)
+
+        block = index - per_panel
+
+        @pl.when(block == 0)
+        def _():
+            give_parts(0)
+
+        @pl.when(block == per_panel // 8)
+        def _():
+            give_sums(0)
+
+        @pl.when(block == per_panel // 4 - 1)
+        def _():
+            solve(0)
+
+        @pl.when(jnp.logical_and(block >= 0, block < per_panel))
+        def _():
+            panel = reflectors(1, block)
+            add(1, 0, width, dot(panel, panel, 0, 0))
+
+        @pl.when(jnp.logical_and(block >= per_panel // 4, block < per_panel // 2))
+        def _():
+            @pl.loop(0, 4)
+            def _(more):
+                other = (block - per_panel // 4) * 4 + more
+                at = piece(other)
+                current[:, at] = current[:, at] - dot(solved[0], reflectors(0, other), 1, 1)
+
+        @pl.when(jnp.logical_and(block >= per_panel // 2, block < per_panel))
+        def _():
+            for more in range(2):
+                add_inner(1, (block - per_panel // 2) * 2 + more)
+
+    give_parts(1)
+    give_sums(1)
+    solve(1)
 
     def out_copy(block):
         at = piece(block)
@@ -232,8 +281,7 @@
 
     @pl.loop(0, per_panel)
     def _(block):
-        update = dot(solved[0], reflectors(0, block), 1, 1) + dot(
-            solved[1], reflectors(1, block), 1, 1)
+        update = dot_halves(halves(solved[1]), halves(reflectors(1, block)), 1, 1)
         at = piece(block)
         current[:, at] = current[:, at] - update
         out_copy(block).start()
@@ -251,8 +299,9 @@
     for step in range(1, row_n):
         if exchange:
             swap(step).wait_send()
-        part_copy(step).wait_send()
-        full_copy(step).wait_send()
+        for panel in range(PANELS):
+            part_copy(panel, step).wait_send()
+            full_copy(panel, step).wait_send()
 
     @pl.loop(0, per_panel)
     def _(block):
@@ -274,7 +323,7 @@
     flags = jnp.concatenate([order == col, order <= col]).astype(jnp.int32)
     flags = jnp.broadcast_to(
         jnp.pad(flags, (0, 8 - 2 * PANELS))[:, None], (8, width))
-    rows = (PANELS + 1) * width + PANELS * mine_rows
+    rows = width + mine_rows
     share = -(-rows // (8 * row_n)) * 8
     dma = pltpu.SemaphoreType.DMA
     return pl.pallas_call(
@@ -291,13 +340,14 @@
             pltpu.VMEM((PANELS * row_count, width), jnp.float32),
             pltpu.VMEM((row_count, width), jnp.float32),
             pltpu.VMEM((mine_rows, row_count), jnp.float32),
-            pltpu.VMEM((share * row_n, width), jnp.float32),
-            pltpu.VMEM((row_n, share, width), jnp.float32),
-            pltpu.VMEM((share * row_n, width), jnp.float32),
+            pltpu.VMEM((PANELS, share * row_n, width), jnp.float32),
+            pltpu.VMEM((PANELS, row_n, share, width), jnp.float32),
+            pltpu.VMEM((PANELS, share * row_n, width), jnp.float32),
             pltpu.VMEM((PANELS, mine_rows, width), jnp.float32),
             dma((total,)), dma((total,)), dma((total,)), dma((total,)),
-            dma((row_n,)), dma((row_n,)), dma((row_n,)), dma((row_n,)),
             dma((row_n,)), dma((row_n,)),
+            dma((PANELS, row_n)), dma((PANELS, row_n)),
+            dma((PANELS, row_n)), dma((PANELS, row_n)),
             dma, dma, dma((per_panel,)),
         ],
         compiler_params=pltpu.CompilerParams(

time: 463 us -> 427 us (0.922)
  Pallas kernels: 453 us -> 418 us
    pallas_call x1, Pallas kernels: 453 us -> 418 us  [on_device(): pl.pallas_call(functools.partial(kernel, row_n, col_n, chunk, exchange),...]
where the time goes in v2:
time: 427 us
  Pallas kernels  418 us (98%)
  local copies, waits for them, and re-layouts  9.1 us (2%)
    pallas_call x1, Pallas kernels, on_device(): pl.pallas_call(functools.partial(kernel, row_n, col_n, chunk, exchange),...  418 us

profile of v2, /device:TPU:1, one launch (start us, length us, event | category | flops | bytes accessed | tf_op | source)
XLA Modules:
  0.0 427.0 jit_solution(13556945660169819789)
XLA Ops:
  0.0 0.7 rev.3
  0.8 0.1 pad_add_fusion
  0.8 0.7 broadcast_in_dim.2.flag_ref
  1.5 417.8 %shard_map.37 = f32[256,8192]{1,0:T(8,128)} custom-call(f32[32,65536]{1,0:T(8,128)} %eigen_ref.1, f32[8192,256]{1,0:T(8,128)} %house_ref.1, s32[8,256]{1,0:T(8,128)} %broadcast_in_dim.2.flag_ref), custom_call_target="tpu_custom_call" | custom-call | tf_op jit(solution)/shard_map/pallas_call | solution.py:329
  419.3 7.7 %copy.5 = f32[256,8192]{1,0:T(8,128)} copy(f32[256,8192]{1,0:T(8,128)} %shard_map.37) | data formatting | bytes 16777216
  (2 shorter events, 0.0 us)

commit v3 on v2

--- a/solution.py
+++ b/solution.py
@@ -55,10 +55,10 @@
 
 
 def kernel(
-    row_n, col_n, chunk, exchange, eigen_ref, house_ref, flag_ref, out_ref,
+    row_n, col_n, chunk, exchange, eigen_ref, house_ref, flag_ref, held_ref, panel_ref, solved_ref,
     right_buf, left_buf, own, current, acc, parts, full, solved,
     right_send, right_recv, left_send, left_recv,
-    swap_send, swap_recv, part_send, part_recv, full_send, full_recv, own_sem, here_sem, out_sem,
+    swap_send, swap_recv, part_send, part_recv, full_send, full_recv, own_sem, here_sem, held_sem, panel_sem, solved_sem,
 ):
     row = lax.axis_index("row")
     col = lax.axis_index("col")
@@ -157,6 +157,14 @@
         cols = (PANELS - 1 - panel) * width + lax.broadcasted_iota(jnp.int32, stored.shape, 1)
         return jnp.where(rows > cols, stored, jnp.where(rows == cols, 1.0, 0.0))
 
+    def held_copy(block):
+        at = piece(block)
+        return pltpu.make_async_copy(current.at[:, at], held_ref.at[:, at], held_sem.at[block])
+
+    def panel_copy(block):
+        at = piece(block)
+        return pltpu.make_async_copy(own.at[at, :], panel_ref.at[at, :], panel_sem.at[block])
+
     def add(panel, start, size, value):
         acc[panel, start:start + size, :] = acc[panel, start:start + size, :] + value
 
@@ -256,6 +264,8 @@
         @pl.when(jnp.logical_and(block >= 0, block < per_panel))
         def _():
             panel = reflectors(1, block)
+            own[piece(block), :] = panel
+            panel_copy(block).start()
             add(1, 0, width, dot(panel, panel, 0, 0))
 
         @pl.when(jnp.logical_and(block >= per_panel // 4, block < per_panel // 2))
@@ -265,6 +275,7 @@
                 other = (block - per_panel // 4) * 4 + more
                 at = piece(other)
                 current[:, at] = current[:, at] - dot(solved[0], reflectors(0, other), 1, 1)
+                held_copy(other).start()
 
         @pl.when(jnp.logical_and(block >= per_panel // 2, block < per_panel))
         def _():
@@ -275,16 +286,8 @@
     give_sums(1)
     solve(1)
 
-    def out_copy(block):
-        at = piece(block)
-        return pltpu.make_async_copy(current.at[:, at], out_ref.at[:, at], out_sem.at[block])
-
-    @pl.loop(0, per_panel)
-    def _(block):
-        update = dot_halves(halves(solved[1]), halves(reflectors(1, block)), 1, 1)
-        at = piece(block)
-        current[:, at] = current[:, at] - update
-        out_copy(block).start()
+    solved_copy = pltpu.make_async_copy(solved.at[1], solved_ref, solved_sem)
+    solved_copy.start()
 
     @pl.loop(0, total)
     def _(index):
@@ -305,7 +308,14 @@
 
     @pl.loop(0, per_panel)
     def _(block):
-        out_copy(block).wait()
+        held_copy(block).wait()
+        panel_copy(block).wait()
+
+    solved_copy.wait()
+
+
+def update_kernel(held_ref, panel_ref, solved_ref, out_ref):
+    out_ref[...] = held_ref[...] - dot_split(solved_ref[...], panel_ref[...], 1, 1)
 
 
 def on_device(row_n, col_n, eigen_rows, householder, owners):
@@ -326,15 +336,19 @@
     rows = width + mine_rows
     share = -(-rows // (8 * row_n)) * 8
     dma = pltpu.SemaphoreType.DMA
-    return pl.pallas_call(
+    held, panel, solved = pl.pallas_call(
         functools.partial(kernel, row_n, col_n, chunk, exchange),
-        out_shape=jax.ShapeDtypeStruct((mine_rows, row_count), jnp.float32),
+        out_shape=[
+            jax.ShapeDtypeStruct((mine_rows, row_count), jnp.float32),
+            jax.ShapeDtypeStruct((row_count, width), jnp.float32),
+            jax.ShapeDtypeStruct((mine_rows, width), jnp.float32),
+        ],
         in_specs=[
             pl.BlockSpec(memory_space=pl.ANY),
             pl.BlockSpec(memory_space=pl.ANY),
             pl.BlockSpec(memory_space=pltpu.VMEM),
         ],
-        out_specs=pl.BlockSpec(memory_space=pl.ANY),
+        out_specs=[pl.BlockSpec(memory_space=pl.ANY)] * 3,
         scratch_shapes=[
             pltpu.VMEM((PANELS * row_count, width), jnp.float32),
             pltpu.VMEM((PANELS * row_count, width), jnp.float32),
@@ -348,11 +362,24 @@
             dma((row_n,)), dma((row_n,)),
             dma((PANELS, row_n)), dma((PANELS, row_n)),
             dma((PANELS, row_n)), dma((PANELS, row_n)),
-            dma, dma, dma((per_panel,)),
+            dma, dma, dma((per_panel,)), dma((per_panel,)), dma,
         ],
         compiler_params=pltpu.CompilerParams(
             collective_id=0, has_side_effects=True, vmem_limit_bytes=60 * 2**20),
     )(eigen_rows, householder, flags)
+    tile = min(1024, row_count)
+    return pl.pallas_call(
+        update_kernel,
+        out_shape=jax.ShapeDtypeStruct((mine_rows, row_count), jnp.float32),
+        grid=(row_count // tile,),
+        in_specs=[
+            pl.BlockSpec((mine_rows, tile), lambda i: (0, i)),
+            pl.BlockSpec((tile, width), lambda i: (i, 0)),
+            pl.BlockSpec((mine_rows, width), lambda i: (0, 0)),
+        ],
+        out_specs=pl.BlockSpec((mine_rows, tile), lambda i: (0, i)),
+        compiler_params=pltpu.CompilerParams(vmem_limit_bytes=32 * 2**20),
+    )(held, panel, solved)
 
 
 def solution(mesh):

time: 427 us -> 424 us (level)
    pallas_call x1, Pallas kernels: 418 us -> 408 us  [on_device(): pl.pallas_call(functools.partial(kernel, row_n, col_n, chunk, exchange),...]
    pallas_call x0 -> x1, Pallas kernels: none -> 7.34 us  [on_device(): pl.pallas_call(update_kernel, out_shape=jax.ShapeDtypeStruct((mine_rows,...]
where the time goes in v3:
time: 424 us
  Pallas kernels  415 us (98%)
  local copies, waits for them, and re-layouts  9.12 us (2%)
    pallas_call x1, Pallas kernels, on_device(): pl.pallas_call(functools.partial(kernel, row_n, col_n, chunk, exchange),...  408 us

profile of v3, /device:TPU:1, one launch (start us, length us, event | category | flops | bytes accessed | tf_op | source)
XLA Modules:
  0.0 424.1 jit_solution(6601300223831846393)
XLA Ops:
  0.0 0.7 rev.3
  0.8 0.1 pad_add_fusion
  0.8 0.7 broadcast_in_dim.2.flag_ref
  1.5 407.5 %shard_map.37 = (f32[256,8192]{1,0:T(8,128)}, f32[8192,256]{1,0:T(8,128)}, f32[256,256]{1,0:T(8,128)}) custom-call(f32[32,65536]{1,0:T(8,128)} %eigen_ref.1, f32[8192,256]{1,0:T(8,128)} %house_ref.1, s32[8,256]{1,0:T(8,128)} %broadcast_in_dim.2.flag_ref), custom_call_target="tpu_custom_call" | custom-call | tf_op jit(solution)/shard_map/pallas_call | solution.py:339
  409.1 0.0 copy-start
  409.1 3.4 copy-done
  412.4 0.0 copy-start.1
  412.4 3.4 copy-done.1
  415.8 0.0 copy-start.2
  415.8 0.9 copy-done.2
  416.8 7.3 %shard_map.38 = f32[256,8192]{1,0:T(8,128)} custom-call(f32[256,8192]{1,0:T(8,128)S(1)} %copy-done, f32[8192,256]{1,0:T(8,128)S(1)} %copy-done.1, f32[256,256]{1,0:T(8,128)S(1)} %copy-done.2), custom_call_target="tpu_custom_call" | custom-call | tf_op jit(solution)/shard_map/pallas_call | solution.py:371
  (2 shorter events, 0.0 us)
Async XLA Ops:
  409.1 3.4 copy-start
  412.4 3.4 copy-start.1
  415.8 0.9 copy-start.2
